TPU v7x, 32 devices: a whole 2x2x4 slice. The times are simulated.
32 devices in a mesh: dp: 8 (over y, x, core), mp: 4 (over z).
Axes of the slice: x: 2, y: 2, z: 4, core: 2. Of those that a mesh axis runs over, the one named last changes fastest.
Arguments:
- tokens: bfloat16 [12288, 768], P('dp'), may hold values from -6 to 6
- alignment: int32 [24, 128], P('dp'), may hold values from 0 to 383, as said below
- segment_count: int32 [24], P('dp'), may hold values from 5 to 128, as said below
- text_mask: int32 [24, 384], P('dp'), may hold values from 0 to 1, as said below
- cotangent: bfloat16 [12288, 768], P('dp'), may hold values from -6 to 6
- attention_master: float32 [768, 4, 768], P('dp', None, 'mp')
- attention_moment: float32 [768, 4, 768], P('dp', None, 'mp')
- attention_average: float32 [768, 4, 768], P('dp', None, 'mp')
- feedforward_master: float32 [768, 2, 3072], P('dp', None, 'mp')
- feedforward_moment: float32 [768, 2, 3072], P('dp', None, 'mp')
- feedforward_average: float32 [768, 2, 3072], P('dp', None, 'mp')
- shared_master: float32 [768, 6], P('dp')
- shared_moment: float32 [768, 6], P('dp')
- shared_average: float32 [768, 6], P('dp')
- split_master: float32 [768, 6], P('mp')
- split_moment: float32 [768, 6], P('mp')
- split_average: float32 [768, 6], P('mp')
Outputs:
- layer_output: bfloat16 [12288, 768], P('dp')
- input_gradient: float32 [12288, 768], P('dp')
- attention_velocity: float32 [768, 4, 768], P('dp', None, 'mp')
- attention_updated: float32 [768, 4, 768], P('dp', None, 'mp')
- attention_averaged: float32 [768, 4, 768], P('dp', None, 'mp')
- attention_rounded: bfloat16 [768, 4, 768], P('dp', None, 'mp')
- feedforward_velocity: float32 [768, 2, 3072], P('dp', None, 'mp')
- feedforward_updated: float32 [768, 2, 3072], P('dp', None, 'mp')
- feedforward_averaged: float32 [768, 2, 3072], P('dp', None, 'mp')
- feedforward_rounded: bfloat16 [768, 2, 3072], P('dp', None, 'mp')
- shared_velocity: float32 [768, 6], P('dp')
- shared_updated: float32 [768, 6], P('dp')
- shared_averaged: float32 [768, 6], P('dp')
- shared_rounded: bfloat16 [768, 6], P('dp')
- split_velocity: float32 [768, 6], P('mp')
- split_updated: float32 [768, 6], P('mp')
- split_averaged: float32 [768, 6], P('mp')
- split_rounded: bfloat16 [768, 6], P('mp')
Inputs may be any that keep to these rules, and one draw needn't show every extreme that they name: alignment[d, j] is less than the number of ones in row d of text_mask. `segment_count`: at least one document holds 128 live segment slots. `text_mask`: each row is ones followed by zeros, with at least 96 ones; some row is all ones.
All inputs are finite; a program needn't handle non-finite values.
Results may differ from a plain program's by a relative error of at most 0.02.
Values may be sent and summed in bfloat16 or wider, within the bound.
A program may use at most 128 MiB of HBM per device.

v0:
```python
from functools import partial

import jax
import jax.numpy as jnp
from jax import lax
from jax.sharding import PartitionSpec as P

HEAD_DIM = 64


EPS = 1e-05
MOMENTUM = 0.9
AVERAGE = 0.75
ATTENTION_RATES = (4e-05, 4e-05, 4e-05, 0.01)
FEEDFORWARD_RATES = (0.0002, 4e-05)
SHARED_RATE = 0.0006
SPLIT_RATES = (0.0004, 0.0003, 0.0017, 0.0017, 0.0017, 0.0017)
HIGHEST_MODE = lax.Precision.HIGHEST


def contract_last(left, right):
    return lax.dot_general(
        left, right, (((1,), (1,)), ((), ())), preferred_element_type=jnp.float32
    )


def contract_rows(left, right):
    return lax.dot_general(
        left, right, (((0,), (0,)), ((), ())), preferred_element_type=jnp.float32
    )


def layer_norm(value, gain, shift):
    center = value - jnp.mean(value, axis=-1, keepdims=True)
    factor = lax.rsqrt(jnp.mean(center * center, axis=-1, keepdims=True) + EPS)
    normed = center * factor
    return (normed * gain + shift, normed, factor)


def norm_back(incoming, normed, factor, gain):
    scaled = incoming * gain
    inner_part = (
        scaled
        - jnp.mean(scaled, axis=-1, keepdims=True)
        - normed * jnp.mean(scaled * normed, axis=-1, keepdims=True)
    )
    return (factor * inner_part, jnp.sum(incoming * normed, axis=0), jnp.sum(incoming, axis=0))


def masked_scores(queries, key_rows, valid_keys):
    scores = jnp.einsum(
        "qhd,khd->hqk", queries, key_rows, preferred_element_type=jnp.float32
    ) * HEAD_DIM ** (-0.5)
    return jnp.where(valid_keys[None, None, :], scores, -1e30)


def attend(pieces):
    queries, key_rows, value_rows, valid_keys = pieces
    scores = masked_scores(queries, key_rows, valid_keys)
    row_max = jnp.max(scores, axis=-1, keepdims=True)
    exponent = jnp.exp(scores - row_max)
    row_total = jnp.sum(exponent, axis=-1, keepdims=True)
    probability = (exponent / row_total).astype(jnp.bfloat16)
    context = jnp.einsum(
        "hqk,khd->qhd", probability, value_rows, preferred_element_type=jnp.float32
    )
    return (context.astype(jnp.bfloat16), row_max + jnp.log(row_total))


def attend_back(pieces):
    queries, key_rows, value_rows, valid_keys, upstream, logsum = pieces
    scores = masked_scores(queries, key_rows, valid_keys)
    probability = jnp.exp(scores - logsum)
    grad_values = jnp.einsum(
        "hqk,qhd->khd",
        probability.astype(jnp.bfloat16),
        upstream,
        preferred_element_type=jnp.float32,
    )
    grad_probs = jnp.einsum(
        "qhd,khd->hqk", upstream, value_rows, preferred_element_type=jnp.float32
    )
    row_delta = jnp.sum(probability * grad_probs, axis=-1, keepdims=True)
    grad_scores = (probability * (grad_probs - row_delta)).astype(jnp.bfloat16)
    grad_queries = jnp.einsum(
        "hqk,khd->qhd", grad_scores, key_rows, preferred_element_type=jnp.float32
    ) * HEAD_DIM ** (-0.5)
    grad_keys = jnp.einsum(
        "hqk,qhd->khd", grad_scores, queries, preferred_element_type=jnp.float32
    ) * HEAD_DIM ** (-0.5)
    return (
        grad_queries.astype(jnp.bfloat16),
        grad_keys.astype(jnp.bfloat16),
        grad_values.astype(jnp.bfloat16),
    )


def renew(master, moment, average, gradient, rates):
    velocity = MOMENTUM * moment + gradient
    updated = master - rates * (gradient + MOMENTUM * velocity)
    averaged = AVERAGE * average + (1.0 - AVERAGE) * updated
    return (velocity, updated, averaged, updated.astype(jnp.bfloat16))


def shards(
    tokens,
    alignment,
    segment_count,
    text_mask,
    cotangent,
    attention_master,
    attention_moment,
    attention_average,
    feedforward_master,
    feedforward_moment,
    feedforward_average,
    shared_master,
    shared_moment,
    shared_average,
    split_master,
    split_moment,
    split_average,
):
    documents, slot_count = alignment.shape
    text_rows = text_mask.shape[1]
    document_rows = text_rows + slot_count
    model_width = tokens.shape[1]
    local_width = split_master.shape[0]
    local_heads = local_width // HEAD_DIM
    row_count = documents * document_rows
    attention_full, feedforward_full, shared_full = (
        lax.all_gather(attention_master.astype(jnp.bfloat16), "dp", axis=0, tiled=True),
        lax.all_gather(feedforward_master.astype(jnp.bfloat16), "dp", axis=0, tiled=True),
        lax.all_gather(shared_master.astype(jnp.bfloat16), "dp", axis=0, tiled=True),
    )
    shared = shared_full.astype(jnp.float32)
    split_bias = lax.optimization_barrier(split_master.astype(jnp.bfloat16)).astype(jnp.float32)
    live_slots = (
        lax.broadcasted_iota(jnp.int32, (documents, slot_count), 1) < segment_count[:, None]
    )
    valid_keys = jnp.concatenate([text_mask > 0, live_slots], axis=1)
    text_index = lax.broadcasted_iota(jnp.int32, (documents, slot_count, text_rows), 2)
    pick_table = ((alignment[:, :, None] == text_index) & live_slots[:, :, None]).astype(
        jnp.bfloat16
    )
    inputs = tokens.reshape(documents, document_rows, model_width)
    taken_rows = jnp.einsum(
        "dst,dtw->dsw", pick_table, inputs[:, :text_rows], preferred_element_type=jnp.float32
    )
    layer_in = jnp.concatenate(
        [
            inputs[:, :text_rows].astype(jnp.float32),
            inputs[:, text_rows:].astype(jnp.float32) + taken_rows,
        ],
        axis=1,
    ).reshape(row_count, model_width)
    rows_in = layer_in.astype(jnp.bfloat16)
    project_weights = attention_full[:, :3].reshape(model_width, 3 * local_width)
    project_bias = jnp.concatenate(
        [split_bias[:, 0], jnp.zeros_like(split_bias[:, 0]), split_bias[:, 1]]
    )
    projected = (
        jnp.dot(rows_in, project_weights, preferred_element_type=jnp.float32) + project_bias
    ).astype(jnp.bfloat16)
    projected = projected.reshape(documents, document_rows, 3, local_heads, HEAD_DIM)
    queries = projected[:, :, 0]
    key_rows = projected[:, :, 1]
    value_rows = projected[:, :, 2]
    context, logsum = lax.map(attend, (queries, key_rows, value_rows, valid_keys))
    context_rows = context.reshape(row_count, local_width)
    joined = lax.psum(
        contract_last(context_rows, attention_full[:, 3]).astype(jnp.bfloat16), "mp"
    ).astype(jnp.float32)
    mixed = layer_in + joined + shared[:, 0]
    first_norm, normed_one, factor_one = layer_norm(mixed, shared[:, 1], shared[:, 2])
    hidden_in = first_norm.astype(jnp.bfloat16)
    inner_pre = jnp.dot(
        hidden_in, feedforward_full[:, 0], preferred_element_type=jnp.float32
    ) + split_bias[:, 2:].reshape(-1)
    active = jax.nn.gelu(inner_pre, approximate=False).astype(jnp.bfloat16)
    down_sum = lax.psum(
        contract_last(active, feedforward_full[:, 1]).astype(jnp.bfloat16), "mp"
    ).astype(jnp.float32)
    second = first_norm + down_sum + shared[:, 5]
    output, normed_two, factor_two = layer_norm(second, shared[:, 3], shared[:, 4])
    grad_second, grad_gain_two, grad_shift_two = norm_back(
        cotangent.astype(jnp.float32), normed_two, factor_two, shared[:, 3]
    )
    grad_down = grad_second.astype(jnp.bfloat16)
    grad_active = jnp.dot(grad_down, feedforward_full[:, 1], preferred_element_type=jnp.float32)
    gelu_value, gelu_pull = jax.vjp(partial(jax.nn.gelu, approximate=False), inner_pre)
    grad_inner = gelu_pull(grad_active)[0].astype(jnp.bfloat16)
    feedforward_grad = jnp.stack(
        [contract_rows(hidden_in, grad_inner), contract_rows(grad_down, active)], axis=1
    )
    grad_first = grad_second + lax.psum(
        contract_last(grad_inner, feedforward_full[:, 0]).astype(jnp.bfloat16), "mp"
    ).astype(jnp.float32)
    grad_mixed, grad_gain_one, grad_shift_one = norm_back(
        grad_first, normed_one, factor_one, shared[:, 1]
    )
    grad_joined = grad_mixed.astype(jnp.bfloat16)
    output_grad = contract_rows(grad_joined, context_rows)
    grad_context = jnp.dot(
        grad_joined, attention_full[:, 3], preferred_element_type=jnp.float32
    ).astype(jnp.bfloat16)
    upstream = grad_context.reshape(documents, document_rows, local_heads, HEAD_DIM)
    grad_queries, grad_keys, grad_values = lax.map(
        attend_back, (queries, key_rows, value_rows, valid_keys, upstream, logsum)
    )
    query_rows = grad_queries.reshape(row_count, local_width)
    value_grad_rows = grad_values.reshape(row_count, local_width)
    grad_project = jnp.concatenate(
        [query_rows, grad_keys.reshape(row_count, local_width), value_grad_rows], axis=1
    )
    project_grad = contract_rows(rows_in, grad_project).reshape(model_width, 3, local_width)
    attention_grad = jnp.concatenate([project_grad, output_grad[:, None, :]], axis=1)
    grad_layer_in = grad_mixed + lax.psum(
        contract_last(grad_project, project_weights).astype(jnp.bfloat16), "mp"
    ).astype(jnp.float32)
    shared_grad = jnp.stack(
        [
            jnp.sum(grad_mixed, axis=0),
            grad_gain_one,
            grad_shift_one,
            grad_gain_two,
            grad_shift_two,
            jnp.sum(grad_second, axis=0),
        ],
        axis=1,
    )
    split_grad = jnp.concatenate(
        [
            jnp.sum(query_rows, axis=0, dtype=jnp.float32)[:, None],
            jnp.sum(value_grad_rows, axis=0, dtype=jnp.float32)[:, None],
            jnp.sum(grad_inner, axis=0, dtype=jnp.float32).reshape(local_width, 4),
        ],
        axis=1,
    )
    grad_documents = grad_layer_in.reshape(documents, document_rows, model_width)
    moved_rows = jnp.einsum(
        "dst,dsw->dtw",
        pick_table.astype(jnp.float32),
        grad_documents[:, text_rows:],
        precision=HIGHEST_MODE,
        preferred_element_type=jnp.float32,
    )
    input_gradient = jnp.concatenate(
        [grad_documents[:, :text_rows] + moved_rows, grad_documents[:, text_rows:]], axis=1
    ).reshape(row_count, model_width)
    attention_sum, feedforward_sum, shared_sum = (
        lax.psum_scatter(attention_grad, "dp", scatter_dimension=0, tiled=True),
        lax.psum_scatter(feedforward_grad, "dp", scatter_dimension=0, tiled=True),
        lax.psum_scatter(shared_grad, "dp", scatter_dimension=0, tiled=True),
    )
    split_sum = lax.psum(split_grad, "dp")
    attention_new = renew(
        attention_master,
        attention_moment,
        attention_average,
        attention_sum,
        jnp.asarray(ATTENTION_RATES, jnp.float32).reshape(1, 4, 1),
    )
    feedforward_new = renew(
        feedforward_master,
        feedforward_moment,
        feedforward_average,
        feedforward_sum,
        jnp.asarray(FEEDFORWARD_RATES, jnp.float32).reshape(1, 2, 1),
    )
    shared_new = renew(shared_master, shared_moment, shared_average, shared_sum, SHARED_RATE)
    split_new = renew(
        split_master,
        split_moment,
        split_average,
        split_sum,
        jnp.asarray(SPLIT_RATES, jnp.float32).reshape(1, 6),
    )
    return (
        output.astype(jnp.bfloat16),
        input_gradient,
        attention_new[0],
        attention_new[1],
        attention_new[2],
        attention_new[3],
        feedforward_new[0],
        feedforward_new[1],
        feedforward_new[2],
        feedforward_new[3],
        shared_new[0],
        shared_new[1],
        shared_new[2],
        shared_new[3],
        split_new[0],
        split_new[1],
        split_new[2],
        split_new[3],
    )


def solution(mesh):
    in_specs = (
        P("dp", None),
        P("dp", None),
        P("dp"),
        P("dp", None),
        P("dp", None),
        P("dp", None, "mp"),
        P("dp", None, "mp"),
        P("dp", None, "mp"),
        P("dp", None, "mp"),
        P("dp", None, "mp"),
        P("dp", None, "mp"),
        P("dp", None),
        P("dp", None),
        P("dp", None),
        P("mp", None),
        P("mp", None),
        P("mp", None),
    )
    out_specs = (
        P("dp", None),
        P("dp", None),
        P("dp", None, "mp"),
        P("dp", None, "mp"),
        P("dp", None, "mp"),
        P("dp", None, "mp"),
        P("dp", None, "mp"),
        P("dp", None, "mp"),
        P("dp", None, "mp"),
        P("dp", None, "mp"),
        P("dp", None),
        P("dp", None),
        P("dp", None),
        P("dp", None),
        P("mp", None),
        P("mp", None),
        P("mp", None),
        P("mp", None),
    )
    return jax.shard_map(shards, mesh=mesh, in_specs=in_specs, out_specs=out_specs, check_vma=False)
```

profile of v0, /device:TPU:0, one launch (start us, length us, event | category | flops | bytes accessed | tf_op | source)
XLA Modules:
  0.0 728.4 jit_solution(8136103924556645693)
XLA Ops:
  17.3 21.6 %all-gather.4.cloned.1.call-done = bf16[768,4,192]{2,1,0:T(4,128)(2,1)} async-done(((bf16[96,4,192]{2,1,0:T(4,128)(2,1)}), bf16[768,4,192]{2,1,0:T(4,128)(2,1)}) %all-gather.4.cloned.1.call-update) | async-done | bytes 1179664 | tf_op jit(solution)/shard_map/all_gather | solution.py:132
  38.9 3.4 copy.232
  42.3 4.7 add_convert_fusion.2
  47.0 5.2 reshape.194
  58.5 17.1 %while.26 = (s32[]{:T(128)}, bf16[3,512,3,64]{1,3,2,0:T(8,128)(2,1)}, f32[3,3,512,1]{2,1,3,0:T(4,128)}, bf16[3,512,3,64]{1,3,2,0:T(8,128)(2,1)}, pred[3,512]{1,0...) while((s32[]{:T(128)}, ...), condition=%wide.region_3.4_spmd, body=%wide.region_0.3_spmd.sunk | while | flops 210860544 | bytes 10280025 | solution.py:169
  78.1 3.1 slice.95
  84.1 3.4 convolution_convert_fusion.3
  89.4 9.2 %all-gather = bf16[8,96,6]{1,2,0:T(8,128)(2,1)S(1)} all-gather(bf16[1,96,6]{1,2,0:T(8,128)(2,1)S(1)} %convert_bitcast_fusion), channel_id=1, replica_groups=mesh['dp'=8,'mp'=4] {'dp'}, dimensions={0}, use_global_device_ids=true | all-gather | bytes 10368 | tf_op jit(solution)/shard_map/all_gather | solution.py:134
  104.6 3.8 pad_maximum_fusion
  108.4 74.9 %all-reduce.5.cloned.1.call-done = bf16[1536,768]{1,0:T(8,128)(2,1)} async-done(((bf16[1536,768]{1,0:T(8,128)(2,1)}), bf16[1536,768]{1,0:T(8,128)(2,1)}) %all-reduce.5.cloned.1.call-update) | async-done | bytes 2359312 | tf_op jit(solution)/shard_map/psum | solution.py:171
  183.3 3.8 fusion.103
  190.3 23.6 %all-gather.6.cloned.1.call-done = bf16[768,2,768]{2,0,1:T(8,128)(2,1)} async-done(((bf16[96,2,768]{2,0,1:T(8,128)(2,1)}), bf16[768,2,768]{2,0,1:T(8,128)(2,1)}) %all-gather.6.cloned.1.call-update) | async-done | bytes 2359312 | tf_op jit(solution)/shard_map/all_gather | solution.py:133
  213.8 14.3 %multiply_convert_fusion.1 = (bf16[1536,768]{1,0:T(8,128)(2,1)S(1)}, f32[1536,768]{1,0:T(8,128)}, f32[1536,768]{1,0:T(8,128)}) fusion(f32[768]{0:T(1024)S(1)} %copy-done.35, bf16[1536,768]{1,0:T(8,128)(2,1)S(1)} %fusion.68, bf16[768,2,768]{2,0,1:T(8,128)(2,1)} %all-gather.6.cloned.1.call-done), kind=kOutput, calls=%fused_computation.87 | convolution fusion | flops 1889796096 | bytes 15338496 | tf_op jit(solution)/shard_map/dot_general | solution.py:177
  229.6 3.5 convolution_convert_fusion.2
  233.6 95.2 %all-reduce.7.cloned.1.call-done = bf16[1536,768]{1,0:T(8,128)(2,1)} async-done(((bf16[1536,768]{1,0:T(8,128)(2,1)}), bf16[1536,768]{1,0:T(8,128)(2,1)}) %all-reduce.7.cloned.1.call-update) | async-done | bytes 2359312 | tf_op jit(solution)/shard_map/psum | solution.py:181
  328.8 4.1 fusion.101
  340.3 5.1 convert_reduce_fusion.1
  346.7 3.5 convolution_convert_fusion.1
  351.6 93.4 %all-reduce.9.cloned.1.call-done = bf16[1536,768]{1,0:T(8,128)(2,1)} async-done(((bf16[1536,768]{1,0:T(8,128)(2,1)}), bf16[1536,768]{1,0:T(8,128)(2,1)}) %all-reduce.9.cloned.1.call-update) | async-done | bytes 2359312 | tf_op jit(solution)/shard_map/psum | solution.py:196
  445.0 7.3 %multiply_reduce_fusion.1 = (f32[768]{0:T(1024)}, f32[1536]{0:T(1024)S(1)}, f32[1536]{0:T(1024)S(1)}, f32[768]{0:T(1024)S(1)}, f32[768]{0:T(1024)S(1)}) fusion(f32[1536,768]{1,0:T(8,128)} %copy-done, f32[1536]{0:T(1024)S(1)} %add_rsqrt_fusion.1, f32[1536]{0:T(1024)S(1)} %broadcast_multiply_fusion.5, f32[1536,768]{1,0:T(8,128)} %copy-done.2, ...), kind=kLoop, calls=%fused_computation.78 | loop fusion | flops 14150400 | bytes 11833344 | tf_op jit(solution)/shard_map/reduce_sum | solution.py:47
  452.4 5.3 fusion.98
  461.6 17.5 %while.27 = (s32[]{:T(128)}, bf16[3,512,3,64]{1,3,2,0:T(8,128)(2,1)S(1)}, bf16[3,512,3,64]{1,3,2,0:T(8,128)(2,1)S(1)}, bf16[3,512,3,64]{1,3,2,0:T(8,128)(2,1)S(1...) while((s32[]{:T(128)}, ...), condition=%wide.region_17.18_spmd, body=%wide.region_15.17_spmd.sunk | while | flops 510884352 | bytes 25598580 | solution.py:208
  485.1 3.5 convolution_convert_fusion
  488.9 3.2 convolution_bitcast_fusion.2
  495.8 3.3 copy.230
  499.2 3.9 convolution_bitcast_fusion.1
  503.2 4.5 convolution_bitcast_fusion
  513.2 14.0 %psum.39 = f32[192,6]{0,1:T(8,128)S(1)} all-reduce(f32[192,6]{0,1:T(8,128)S(1)} %pad_maximum_fusion.4), channel_id=1, replica_groups=mesh['dp'=8,'mp'=4] {'dp'}, use_global_device_ids=true, to_apply=%region_31.32 | all-reduce | flops 1152 | bytes 9216 | tf_op jit(solution)/shard_map/psum | solution.py:256
  530.6 82.0 %all-reduce.11.cloned.1.call-done = bf16[1536,768]{1,0:T(8,128)(2,1)} async-done(((bf16[1536,768]{1,0:T(8,128)(2,1)}), bf16[1536,768]{1,0:T(8,128)(2,1)}) %all-reduce.11.cloned.1.call-update) | async-done | bytes 2359312 | tf_op jit(solution)/shard_map/psum | solution.py:218
  612.6 3.6 convert_add_fusion
  620.5 37.1 %reduce-scatter.10.cloned.1.call-done = f32[96,768]{1,0:T(8,128)} async-done(((f32[768,768]{1,0:T(8,128)}), f32[96,768]{1,0:T(8,128)}) %reduce-scatter.10.cloned.1.call-update) | async-done | bytes 294928
  662.5 52.7 %reduce-scatter.8.cloned.1.call-done = f32[96,2,768]{2,0,1:T(8,128)} async-done(((f32[768,2,768]{2,0,1:T(8,128)}), f32[96,2,768]{2,0,1:T(8,128)}) %reduce-scatter.8.cloned.1.call-update) | async-done | bytes 589840 | tf_op jit(solution)/shard_map/reduce_scatter | solution.py:253
  (259 shorter events, 117.5 us)
Async XLA Ops:
  7.2 31.7 %all-gather.4.cloned.1.call-start = ((), (), s32[]{:S(2)}) async-start(), calls=%async_computation.3 | async-start | bytes 1769472 | tf_op jit(solution)/shard_map/all_gather | solution.py:132
  9.0 174.3 %all-reduce.5.cloned.1.call-start = ((), (), s32[]{:S(2)}) async-start(), calls=%async_computation.4 | async-start | bytes 4718592 | tf_op jit(solution)/shard_map/psum | solution.py:171
  78.1 11.3 %copy-start.29 = (f32[96,6]{0,1:T(8,128)S(1)}, f32[96,6]{0,1:T(8,128)}, u32[]{:S(2)}) copy-start(f32[96,6]{0,1:T(8,128)} %param.35) | copy-start | bytes 6916
  87.5 126.4 %all-gather.6.cloned.1.call-start = ((), (), s32[]{:S(2)}) async-start(), calls=%async_computation.5 | async-start | bytes 2654208 | tf_op jit(solution)/shard_map/all_gather | solution.py:133
  89.4 239.5 %all-reduce.7.cloned.1.call-start = ((), (), s32[]{:S(2)}) async-start(), calls=%async_computation.6 | async-start | bytes 4718592 | tf_op jit(solution)/shard_map/psum | solution.py:181
  187.7 26.1 %copy-start.35 = (f32[768]{0:T(1024)S(1)}, f32[768]{0:T(1024)}, u32[]{:S(2)}) copy-start(f32[768]{0:T(1024)} %add.176) | copy-start | bytes 9220
  190.3 37.9 %copy-start.6 = (bf16[1536,768]{1,0:T(8,128)(2,1)}, bf16[1536,768]{1,0:T(8,128)(2,1)S(1)}, u32[]{:S(2)}) copy-start(bf16[1536,768]{1,0:T(8,128)(2,1)S(1)} %fusion.68) | copy-start | bytes 7077892
  213.8 15.7 %copy-start.43 = (bf16[768,2,768]{2,0,1:T(8,128)(2,1)S(1)}, bf16[768,2,768]{2,0,1:T(8,128)(2,1)}, u32[]{:S(2)}) copy-start(bf16[768,2,768]{2,0,1:T(8,128)(2,1)} %all-gather.6.cloned.1.call-done) | copy-start | bytes 7077892
  229.6 99.3 %copy-start.27 = (f32[768]{0:T(1024)S(1)}, f32[768]{0:T(1024)}, u32[]{:S(2)}) copy-start(f32[768]{0:T(1024)} %get-tuple-element.294) | copy-start | bytes 9220
  233.0 212.0 %all-reduce.9.cloned.1.call-start = ((), (), s32[]{:S(2)}) async-start(), calls=%async_computation.7 | async-start | bytes 4718592 | tf_op jit(solution)/shard_map/psum | solution.py:196
  350.2 178.3 %reduce-scatter.12.cloned.1.call-start = ((), (), s32[]{:S(2)}) async-start(), calls=%async_computation.11 | async-start | bytes 442368
  452.4 7.5 %copy-start.11 = (bf16[768,1,192]{0,2,1:T(8,128)(2,1)S(1)}, bf16[768,1,192]{0,2,1:T(8,128)(2,1)}, u32[]{:S(2)}) copy-start(bf16[768,1,192]{0,2,1:T(8,128)(2,1)} %copy.233) | copy-start | bytes 884740
  461.6 18.2 %copy-start.25 = (f32[768]{0:T(1024)S(1)}, f32[768]{0:T(1024)}, u32[]{:S(2)}) copy-start(f32[768]{0:T(1024)} %get-tuple-element.283) | copy-start | bytes 9220
  481.6 131.1 %all-reduce.11.cloned.1.call-start = ((), (), s32[]{:S(2)}) async-start(), calls=%async_computation.8 | async-start | bytes 4718592 | tf_op jit(solution)/shard_map/psum | solution.py:218
  488.6 168.9 %reduce-scatter.10.cloned.1.call-start = ((), (), s32[]{:S(2)}) async-start(), calls=%async_computation.10 | async-start | bytes 2654208
  499.1 216.1 %reduce-scatter.8.cloned.1.call-start = ((), (), s32[]{:S(2)}) async-start(), calls=%async_computation.9 | async-start | bytes 5308416 | tf_op jit(solution)/shard_map/reduce_scatter | solution.py:253
  510.1 17.1 %copy-start.24 = (f32[192,6]{0,1:T(8,128)S(1)}, f32[192,6]{0,1:T(8,128)}, u32[]{:S(2)}) copy-start(f32[192,6]{0,1:T(8,128)} %param.38) | copy-start | bytes 13828
  510.1 17.1 %copy-start.32 = (f32[192,6]{0,1:T(8,128)S(1)}, f32[192,6]{0,1:T(8,128)}, u32[]{:S(2)}) copy-start(f32[192,6]{0,1:T(8,128)} %param.39) | copy-start | bytes 13828
  510.1 17.1 %copy-start.41 = (f32[6]{0:T(128)S(1)}, f32[6]{0:T(128)}, u32[]{:S(2)}) copy-start(f32[6]{0:T(128)} %constant.152.clone) | copy-start | bytes 76
  510.1 17.8 %copy-start.31 = (f32[192,6]{0,1:T(8,128)S(1)}, f32[192,6]{0,1:T(8,128)}, u32[]{:S(2)}) copy-start(f32[192,6]{0,1:T(8,128)} %param.40) | copy-start | bytes 13828
  510.1 19.2 %copy-start.30 = (f32[96,6]{0,1:T(8,128)S(1)}, f32[96,6]{0,1:T(8,128)}, u32[]{:S(2)}) copy-start(f32[96,6]{0,1:T(8,128)} %param.35) | copy-start | bytes 6916
  510.1 19.2 %copy-start.36 = (f32[96,6]{0,1:T(8,128)S(1)}, f32[96,6]{0,1:T(8,128)}, u32[]{:S(2)}) copy-start(f32[96,6]{0,1:T(8,128)} %param.36) | copy-start | bytes 6916
  510.2 19.8 %copy-start.33 = (f32[96,6]{0,1:T(8,128)S(1)}, f32[96,6]{0,1:T(8,128)}, u32[]{:S(2)}) copy-start(f32[96,6]{0,1:T(8,128)} %param.37) | copy-start | bytes 6916
  527.9 88.3 %copy-start.23 = (f32[192,6]{0,1:T(8,128)}, f32[192,6]{0,1:T(8,128)S(1)}, u32[]{:S(2)}) copy-start(f32[192,6]{0,1:T(8,128)S(1)} %get-tuple-element.333) | copy-start | bytes 13828
  530.0 86.2 %copy-start.28 = (f32[96,6]{0,1:T(8,128)}, f32[96,6]{0,1:T(8,128)S(1)}, u32[]{:S(2)}) copy-start(f32[96,6]{0,1:T(8,128)S(1)} %get-tuple-element.336) | copy-start | bytes 6916
  530.6 85.7 %copy-start.37 = (s32[3,128]{1,0:T(4,128)S(1)}, s32[3,128]{1,0:T(4,128)}, u32[]{:S(2)}) copy-start(s32[3,128]{1,0:T(4,128)} %param.25) | copy-start | bytes 4612
  530.6 85.7 %copy-start.39 = (pred[3,128]{1,0:T(4,128)(4,1)S(1)}, pred[3,128]{1,0:T(4,128)(4,1)}, u32[]{:S(2)}) copy-start(pred[3,128]{1,0:T(4,128)(4,1)} %copy-done.38) | copy-start | bytes 1156
  618.0 40.7 %copy-start.40 = (f32[4]{0:T(128)S(1)}, f32[4]{0:T(128)}, u32[]{:S(2)}) copy-start(f32[4]{0:T(128)} %constant.150.clone) | copy-start | bytes 52
  618.0 41.8 %copy-start.16 = (f32[96,4,192]{0,2,1:T(8,128)S(1)}, f32[96,4,192]{0,2,1:T(8,128)}, u32[]{:S(2)}) copy-start(f32[96,4,192]{0,2,1:T(8,128)} %copy.208) | copy-start | bytes 884740
  620.5 94.8 %copy-start.14 = (f32[96,2,768]{2,1,0:T(2,128)S(1)}, f32[96,2,768]{2,1,0:T(2,128)}, u32[]{:S(2)}) copy-start(f32[96,2,768]{2,1,0:T(2,128)} %param.32) | copy-start | bytes 1769476
  620.5 94.8 %copy-start.42 = (f32[2]{0:T(128)S(1)}, f32[2]{0:T(128)}, u32[]{:S(2)}) copy-start(f32[2]{0:T(128)} %constant.151.clone) | copy-start | bytes 28
  658.8 59.2 %copy-start.18 = (f32[96,2,768]{2,1,0:T(2,128)S(1)}, f32[96,2,768]{2,1,0:T(2,128)}, u32[]{:S(2)}) copy-start(f32[96,2,768]{2,1,0:T(2,128)} %param.34) | copy-start | bytes 1769476
  (28 other events, 79.9 us)
Sparse Core Ops, SparseCore 0:
  10.5 28.3 all-gather.3
  87.6 95.6 all-reduce.4
  185.8 28.0 all-gather.5
  233.2 95.6 all-reduce.6
  350.3 94.6 all-reduce.8
  481.7 32.8 reduce-scatter.11
  516.9 95.6 all-reduce.10
  616.0 41.5 reduce-scatter.9
  661.4 53.8 reduce-scatter.7
where the time goes:
time: 737 us; the launch traced here: 728 us
  waiting for transfers between devices  481 us (65%)
  matrix products  81.4 us (11%)
  local copies, waits for them, and re-layouts  65.1 us (9%)
  other arithmetic  61.7 us (8%)
  blocking collectives  23.2 us (3%)
  between operations  15 us (2%)
    psum x1, waiting for transfers between devices, shards(): lax.psum(contract_last(active, feedforward_full[:, 1]).astype(jnp.bfloat1...  95.2 us
    psum x1, waiting for transfers between devices, shards(): lax.psum(contract_last(grad_inner, feedforward_full[:, 0]).astype(jnp.bfl...  93.4 us
    psum x1, waiting for transfers between devices, shards(): lax.psum(contract_last(grad_project, project_weights).astype(jnp.bfloat16...  82 us
    psum x1, waiting for transfers between devices, shards(): lax.psum(contract_last(context_rows, attention_full[:, 3]).astype(jnp.bfl...  74.9 us
    reduce_scatter x1, waiting for transfers between devices, shards(): lax.psum_scatter(feedforward_grad, 'dp', scatter_dimension=0, tiled=True)  52.7 us
    unnamed x11, waiting for transfers between devices  37.2 us
    unnamed x126, local copies, waits for them, and re-layouts  35.9 us
    all_gather x1, waiting for transfers between devices, shards(): lax.all_gather(feedforward_master.astype(jnp.bfloat16), 'dp', axis=0, til...  23.6 us
  transfers between devices with their start and end apart: 9, of which 8 were waited for; matrix products, arithmetic and copies ran while one was open for 10% of the time, Pallas kernels for 0%

commit v1 on v0

--- a/solution.py
+++ b/solution.py
@@ -3,7 +3,11 @@
 import jax
 import jax.numpy as jnp
 from jax import lax
+from jax.experimental import pallas as pl
+from jax.experimental.pallas import tpu as pltpu
 from jax.sharding import PartitionSpec as P
+
+MESH = pl.DeviceIdType.MESH
 
 HEAD_DIM = 64
 
@@ -102,7 +106,7 @@
     return (velocity, updated, averaged, updated.astype(jnp.bfloat16))
 
 
-def shards(
+def general_shards(
     tokens,
     alignment,
     segment_count,
@@ -298,6 +302,550 @@
     )
 
 
+def place():
+    dp, z = lax.axis_index("dp"), lax.axis_index("mp")
+    return z, lax.div(dp, 4), lax.rem(lax.div(dp, 2), 2), lax.rem(dp, 2)
+
+
+def device(z, y, x, c):
+    return (y * 4 + x * 2 + c, z)
+
+
+def nearest_level(z, k):
+    low, high = lax.rem(z, 2), lax.div(z, 2)
+    if k == 0:
+        return z
+    if k == 1:
+        return 1 + (2 * high - 1) * low
+    if k == 2:
+        return 2 + high * (1 - 2 * low)
+    return 3 - 3 * high
+
+
+def greet(z, y, x, c):
+    barrier = pltpu.get_barrier_semaphore()
+    partners = [device(z, y, x, 1 - c), device(z, y, 1 - x, c), device(z, 1 - y, x, c)]
+    partners += [device(lax.rem(z + k, 4), y, x, c) for k in (1, 2, 3)]
+    for partner in partners:
+        pl.semaphore_signal(barrier, inc=1, device_id=partner, device_id_type=MESH)
+    pl.semaphore_wait(barrier, len(partners))
+
+
+def remote(source, target, send, recv, to):
+    return pltpu.make_async_remote_copy(
+        src_ref=source, dst_ref=target, send_sem=send, recv_sem=recv, device_id=to, device_id_type=MESH
+    )
+
+
+def when(condition, action):
+    pl.when(condition)(action)
+
+
+def gather_kernel(
+    own_ref, small_ref, full_ref, plane_ref, line_ref,
+    line_send, line_recv, first_send, first_recv, second_send, second_recv, pair_send, pair_recv,
+    tiny_send, tiny_recv, own_sem, tiny_own,
+):
+    z, y, x, c = place()
+    greet(z, y, x, c)
+    up, down = device(z + 1, y, x, c), device(z - 1, y, x, c)
+    across_x, across_y, pair = device(z, y, 1 - x, c), device(z, 1 - y, x, c), device(z, y, x, 1 - c)
+
+    def line_copy(t, level, source, way):
+        return remote(
+            source, full_ref.at[t, level, y, x, c], line_send.at[t, level, way], line_recv.at[t, level],
+            up if way == 0 else down,
+        )
+
+    own_copies = []
+    for t in range(3):
+        when(z < 3, lambda t=t: line_copy(t, z, own_ref.at[t], 0).start())
+        when(z > 0, lambda t=t: line_copy(t, z, own_ref.at[t], 1).start())
+        copy = pltpu.make_async_copy(own_ref.at[t], full_ref.at[t, z, y, x, c], own_sem.at[t])
+        copy.start()
+        own_copies.append(copy)
+
+    tiny = [pltpu.make_async_copy(small_ref, plane_ref.at[y, x, c], tiny_own.at[0]),
+            pltpu.make_async_copy(small_ref, line_ref.at[z], tiny_own.at[1])]
+    for copy in tiny:
+        copy.start()
+    far = [
+        remote(small_ref, line_ref.at[z], tiny_send.at[k], tiny_recv.at[k], device(lax.rem(z + k, 4), y, x, c))
+        for k in (1, 2, 3)
+    ]
+    for copy in far:
+        copy.start()
+    for copy in tiny:
+        copy.wait()
+    tiny_steps = [
+        remote(plane_ref.at[y, x, c], plane_ref.at[y, x, c], tiny_send.at[4], tiny_recv.at[4], across_x),
+        remote(plane_ref.at[y, :, c], plane_ref.at[y, :, c], tiny_send.at[5], tiny_recv.at[5], across_y),
+        remote(plane_ref.at[:, :, c], plane_ref.at[:, :, c], tiny_send.at[6], tiny_recv.at[6], pair),
+    ]
+
+    def first_copy(t, k):
+        level = nearest_level(z, k)
+        block = full_ref.at[t, level, y, x, c]
+        return remote(
+            own_ref.at[t] if k == 0 else block, block, first_send.at[t, k], first_recv.at[t, k],
+            across_x if (t + k) % 2 == 0 else across_y,
+        )
+
+    def second_copy(t, k):
+        level = nearest_level(z, k)
+        if (t + k) % 2 == 0:
+            block, to = full_ref.at[t, level, y, :, c], across_y
+        else:
+            block, to = full_ref.at[t, level, :, x, c], across_x
+        return remote(block, block, second_send.at[t, k], second_recv.at[t, k], to)
+
+    def pair_copy(t, k):
+        block = full_ref.at[t, nearest_level(z, k), :, :, c]
+        return remote(block, block, pair_send.at[t, k], pair_recv.at[t, k], pair)
+
+    def arrive(t, k):
+        if k > 0:
+            level = nearest_level(z, k)
+            block = full_ref.at[t, level, y, x, c]
+            line_copy(t, level, block, 0).wait_recv()
+            when((level < z) & (z < 3), lambda: line_copy(t, level, block, 0).start())
+            when((level > z) & (z > 0), lambda: line_copy(t, level, block, 1).start())
+        first_copy(t, k).start()
+
+    units = [(t, k) for t in range(3) for k in range(4)]
+    count = len(units)
+    for step in range(count + 3):
+        if step < count:
+            arrive(*units[step])
+        if step < 3:
+            tiny_steps[step].start()
+        if 0 <= step - 1 < count:
+            t, k = units[step - 1]
+            first_copy(t, k).wait_recv()
+            if k == 0:
+                own_copies[t].wait()
+            second_copy(t, k).start()
+        if 0 <= step - 2 < count:
+            second_copy(*units[step - 2]).wait_recv()
+            pair_copy(*units[step - 2]).start()
+        if 0 <= step - 3 < count:
+            pair_copy(*units[step - 3]).wait_recv()
+        if step < 3:
+            tiny_steps[step].wait_recv()
+    for copy in far:
+        copy.wait()
+    for copy in tiny_steps:
+        copy.wait_send()
+    for t, k in units:
+        level = nearest_level(z, k)
+        block = full_ref.at[t, level, y, x, c]
+        if k == 0:
+            when(z < 3, lambda t=t: line_copy(t, z, own_ref.at[t], 0).wait_send())
+            when(z > 0, lambda t=t: line_copy(t, z, own_ref.at[t], 1).wait_send())
+        else:
+            when((level < z) & (z < 3), lambda t=t, level=level, block=block: line_copy(t, level, block, 0).wait_send())
+            when((level > z) & (z > 0), lambda t=t, level=level, block=block: line_copy(t, level, block, 1).wait_send())
+        first_copy(t, k).wait_send()
+        second_copy(t, k).wait_send()
+        pair_copy(t, k).wait_send()
+
+
+def gather(own, small):
+    dma = pltpu.SemaphoreType.DMA
+    return pl.pallas_call(
+        gather_kernel,
+        out_shape=(
+            jax.ShapeDtypeStruct((3, 4, 2, 2, 2, 96, 768), jnp.bfloat16),
+            jax.ShapeDtypeStruct((2, 2, 2, 16, 256), jnp.bfloat16),
+            jax.ShapeDtypeStruct((4, 16, 256), jnp.bfloat16),
+        ),
+        in_specs=[pl.BlockSpec(memory_space=pl.ANY)] * 2,
+        out_specs=(pl.BlockSpec(memory_space=pl.ANY),) * 3,
+        scratch_shapes=[
+            dma((3, 4, 2)), dma((3, 4)), dma((3, 4)), dma((3, 4)), dma((3, 4)), dma((3, 4)), dma((3, 4)), dma((3, 4)),
+            dma((7,)), dma((7,)), dma((3,)), dma((2,)),
+        ],
+        compiler_params=pltpu.CompilerParams(collective_id=0, has_side_effects=True),
+        name="gather_weights",
+    )(own, small)
+
+
+SOURCES = (0, 2, 3)
+LEVEL_ORDER = (0, 3, 1, 2)
+PIECES = 4
+
+
+def reduce_kernel(
+    grads_ref, small_ref, text_ref, back_ref,
+    sum_ref, small_sum_ref, text_all, back_all,
+    total, pair_in, first_in, second_in, line_in, small_total, small_in, line_small,
+    pair_send, pair_recv, first_send, first_recv, second_send, second_recv, line_send, line_recv,
+    small_send, small_recv, cast_send, cast_recv, cast_own,
+):
+    z, y, x, c = place()
+    greet(z, y, x, c)
+    up, down = device(z + 1, y, x, c), device(z - 1, y, x, c)
+    across_x, across_y, pair = device(z, y, 1 - x, c), device(z, 1 - y, x, c), device(z, y, x, 1 - c)
+    rows = text_ref.shape[0] // PIECES
+
+    pieces = [(a, d, p) for p in range(PIECES) for d in range(3) for a in range(2)]
+    arrays = ((text_ref, text_all), (back_ref, back_all))
+
+    def cast_copy(a, d, p, way, first):
+        part = pl.ds(p * rows, rows)
+        target = arrays[a][1].at[d, part]
+        source = arrays[a][0].at[part] if first else target
+        return remote(
+            source, target, cast_send.at[a, d, p, way], cast_recv.at[a, d, p], up if way == 0 else down
+        )
+
+    own_copies = []
+    for a in range(2):
+        for d, start in enumerate(SOURCES):
+            copy = pltpu.make_async_copy(arrays[a][0], arrays[a][1].at[d], cast_own.at[a, d])
+            own_copies.append((start, copy))
+            when(z == start, lambda copy=copy: copy.start())
+    for a, d, p in pieces:
+        start = SOURCES[d]
+        if start < 3:
+            when(z == start, lambda a=a, d=d, p=p: cast_copy(a, d, p, 0, True).start())
+        if start > 0:
+            when(z == start, lambda a=a, d=d, p=p: cast_copy(a, d, p, 1, True).start())
+
+    def relay(a, d, p):
+        start = SOURCES[d]
+
+        def from_below():
+            cast_copy(a, d, p, 0, False).wait_recv()
+            when(z < 3, lambda: cast_copy(a, d, p, 0, False).start())
+
+        def from_above():
+            cast_copy(a, d, p, 1, False).wait_recv()
+            when(z > 0, lambda: cast_copy(a, d, p, 1, False).start())
+
+        if start < 3:
+            when(z > start, from_below)
+        if start > 0:
+            when(z < start, from_above)
+
+    units = [(t, level) for level in LEVEL_ORDER for t in range(3)]
+
+    def along_x(u):
+        return u % 2 == 0
+
+    def pair_copy(u):
+        t, level = units[u]
+        return remote(
+            grads_ref.at[t, level, :, :, 1 - c], pair_in.at[u], pair_send.at[u], pair_recv.at[u], pair
+        )
+
+    def first_copy(u):
+        source = total.at[u, :, 1 - x] if along_x(u) else total.at[u, 1 - y]
+        return remote(
+            source, first_in.at[u], first_send.at[u], first_recv.at[u], across_x if along_x(u) else across_y
+        )
+
+    def second_copy(u):
+        return remote(
+            total.at[u, 1 - y, x] if along_x(u) else total.at[u, y, 1 - x],
+            second_in.at[u], second_send.at[u], second_recv.at[u], across_y if along_x(u) else across_x,
+        )
+
+    def line_copy(u, way):
+        return remote(
+            total.at[u, y, x], line_in.at[u, way], line_send.at[u], line_recv.at[u, way], up if way == 0 else down
+        )
+
+    def line_step(u):
+        t, level = units[u]
+
+        def below():
+            line_copy(u, 0).wait_recv()
+            total[u, y, x] = total[u, y, x] + line_in[u, 0]
+
+        def above():
+            line_copy(u, 1).wait_recv()
+            total[u, y, x] = total[u, y, x] + line_in[u, 1]
+
+        if level > 0:
+            when((z <= level) & (z > 0), below)
+        if level < 3:
+            when((z >= level) & (z < 3), above)
+        when(z < level, lambda: line_copy(u, 0).start())
+        when(z > level, lambda: line_copy(u, 1).start())
+
+        def finish():
+            sum_ref[t] = total[u, y, x].astype(jnp.float32)
+
+        when(z == level, finish)
+
+    small_steps = [
+        remote(small_total.at[i], small_in.at[i], small_send.at[i], small_recv.at[i], to)
+        for i, to in enumerate((pair, across_x, across_y))
+    ]
+    far = [
+        remote(small_total.at[3], line_small.at[z], small_send.at[2 + k], small_recv.at[2 + k], device(lax.rem(z + k, 4), y, x, c))
+        for k in (1, 2, 3)
+    ]
+    for u in range(12):
+        pair_copy(u).start()
+    small_total[0] = small_ref[...]
+    for step in range(12 + 3):
+        if step < 12:
+            t, level = units[step]
+            pair_copy(step).wait_recv()
+            total[step] = grads_ref[t, level, :, :, c] + pair_in[step]
+            first_copy(step).start()
+        if step < 3:
+            small_steps[step].start()
+        if 0 <= step - 1 < 12:
+            u = step - 1
+            first_copy(u).wait_recv()
+            if along_x(u):
+                total[u, :, x] = total[u, :, x] + first_in[u]
+            else:
+                total[u, y] = total[u, y] + first_in[u]
+            second_copy(u).start()
+        if 0 <= step - 2 < 12:
+            u = step - 2
+            second_copy(u).wait_recv()
+            total[u, y, x] = total[u, y, x] + second_in[u]
+        if step < 3:
+            small_steps[step].wait_recv()
+            small_total[step + 1] = small_total[step] + small_in[step]
+            if step == 2:
+                for copy in far:
+                    copy.start()
+                line_small[z] = small_total[3]
+        if 0 <= step - 3 < 12:
+            line_step(step - 3)
+        for piece in pieces[2 * step : 2 * step + 2]:
+            relay(*piece)
+    for copy in far:
+        copy.wait()
+    small_sum_ref[...] = line_small[0] + line_small[1] + line_small[2] + line_small[3]
+    for copy in small_steps:
+        copy.wait_send()
+    for start, copy in own_copies:
+        when(z == start, lambda copy=copy: copy.wait())
+    for u in range(12):
+        t, level = units[u]
+        pair_copy(u).wait_send()
+        first_copy(u).wait_send()
+        second_copy(u).wait_send()
+        when(z < level, lambda u=u: line_copy(u, 0).wait_send())
+        when(z > level, lambda u=u: line_copy(u, 1).wait_send())
+    for a, d, p in pieces:
+        start = SOURCES[d]
+        if start < 3:
+            when((z >= start) & (z < 3), lambda a=a, d=d, p=p: cast_copy(a, d, p, 0, True).wait_send())
+        if start > 0:
+            when((z <= start) & (z > 0), lambda a=a, d=d, p=p: cast_copy(a, d, p, 1, True).wait_send())
+
+
+def reduce_all(grads, small, text, back):
+    dma = pltpu.SemaphoreType.DMA
+    whole = jax.ShapeDtypeStruct((3, 512, 768), jnp.bfloat16)
+    vmem = pl.BlockSpec(memory_space=pltpu.VMEM)
+    hbm = pl.BlockSpec(memory_space=pl.ANY)
+    block = jnp.bfloat16
+    return pl.pallas_call(
+        reduce_kernel,
+        out_shape=(
+            jax.ShapeDtypeStruct((3, 96, 768), jnp.float32),
+            jax.ShapeDtypeStruct((16, 768), jnp.float32),
+            whole,
+            whole,
+        ),
+        in_specs=[vmem, vmem, hbm, hbm],
+        out_specs=(vmem, vmem, hbm, hbm),
+        scratch_shapes=[
+            pltpu.VMEM((12, 2, 2, 96, 768), block),
+            pltpu.VMEM((12, 2, 2, 96, 768), block),
+            pltpu.VMEM((12, 2, 96, 768), block),
+            pltpu.VMEM((12, 96, 768), block),
+            pltpu.VMEM((12, 2, 96, 768), block),
+            pltpu.VMEM((4, 16, 768), jnp.float32),
+            pltpu.VMEM((3, 16, 768), jnp.float32),
+            pltpu.VMEM((4, 16, 768), jnp.float32),
+            dma((12,)), dma((12,)), dma((12,)), dma((12,)), dma((12,)), dma((12,)), dma((12,)), dma((12, 2)),
+            dma((6,)), dma((6,)), dma((2, 3, PIECES, 2)), dma((2, 3, PIECES)), dma((2, 3)),
+        ],
+        compiler_params=pltpu.CompilerParams(
+            collective_id=1, has_side_effects=True, vmem_limit_bytes=58 * 2**20
+        ),
+        name="reduce_gradients",
+    )(grads, small, text, back)
+
+
+def line_shards(
+    tokens,
+    alignment,
+    segment_count,
+    text_mask,
+    cotangent,
+    attention_master,
+    attention_moment,
+    attention_average,
+    feedforward_master,
+    feedforward_moment,
+    feedforward_average,
+    shared_master,
+    shared_moment,
+    shared_average,
+    split_master,
+    split_moment,
+    split_average,
+):
+    documents, slot_count = alignment.shape
+    text_rows = text_mask.shape[1]
+    rows = text_rows + slot_count
+    width = tokens.shape[1]
+    low = jnp.bfloat16
+    level = lax.axis_index("mp")
+    own = jnp.concatenate(
+        [attention_master.reshape(1, 96, 768), jnp.swapaxes(feedforward_master, 0, 1)], axis=0
+    ).astype(low)
+    small = jnp.concatenate(
+        [
+            jnp.pad(shared_master.T, ((0, 0), (0, 160))),
+            jnp.pad(split_master.T, ((0, 4), (0, 64))),
+        ],
+        axis=0,
+    ).astype(low)
+    full, plane_small, line_small = gather(own, small)
+    shared = plane_small.reshape(8, 16, 256)[:, :6, :96].astype(jnp.float32)
+    shared = jnp.swapaxes(shared, 0, 1).reshape(6, 768)
+    split = jnp.swapaxes(line_small[:, 6:12, :192].astype(jnp.float32), 0, 1)
+    bias_q, bias_v = split[0], split[1]
+    bias_up = jnp.stack([split[2], split[3], split[4], split[5]], axis=-1).reshape(4, 768)
+    weights = full.reshape(3, 4, 768, 768)
+    project, w_out = weights[0, :, :, :576], weights[0, :, :, 576:]
+    w_up, w_down = weights[1], weights[2]
+
+    doc = jnp.maximum(level - 1, 0)
+    inputs = lax.dynamic_slice(tokens, (doc * rows, 0), (rows, width))
+    upstream = lax.dynamic_slice(cotangent, (doc * rows, 0), (rows, width)).astype(jnp.float32)
+    upstream = jnp.where(level == 1, 0.0, upstream)
+    slots = lax.dynamic_slice(alignment, (doc, 0), (1, slot_count))[0]
+    live = jnp.arange(slot_count) < lax.dynamic_slice(segment_count, (doc,), (1,))
+    valid = jnp.concatenate([lax.dynamic_slice(text_mask, (doc, 0), (1, text_rows))[0] > 0, live])
+    pick = ((slots[:, None] == jnp.arange(text_rows)[None, :]) & live[:, None]).astype(low)
+    taken = jnp.dot(pick, inputs[:text_rows], preferred_element_type=jnp.float32)
+    layer_in = jnp.concatenate(
+        [inputs[:text_rows].astype(jnp.float32), inputs[text_rows:].astype(jnp.float32) + taken], axis=0
+    )
+    rows_in = layer_in.astype(low)
+
+    def mul(form, left, right):
+        return jnp.einsum(form, left, right, preferred_element_type=jnp.float32)
+
+    bias = jnp.concatenate([bias_q, jnp.zeros_like(bias_q), bias_v], axis=1)
+    projected = (mul("rd,zdc->zrc", rows_in, project) + bias[:, None, :]).astype(low)
+    projected = projected.reshape(4, rows, 3, 3, HEAD_DIM)
+    queries, keys, values = projected[:, :, 0], projected[:, :, 1], projected[:, :, 2]
+    scores = mul("zqhd,zkhd->zhqk", queries, keys) * HEAD_DIM**-0.5
+    scores = jnp.where(valid, scores, -1e30)
+    top = jnp.max(scores, axis=-1, keepdims=True)
+    raised = jnp.exp(scores - top)
+    probs = raised / jnp.sum(raised, axis=-1, keepdims=True)
+    probs_low = probs.astype(low)
+    context = mul("zhqk,zkhd->zqhd", probs_low, values).astype(low).reshape(4, rows, 192)
+    joined = jnp.sum(mul("zrc,zoc->zro", context, w_out).astype(low).astype(jnp.float32), axis=0)
+    mixed = layer_in + joined + shared[0]
+    first_norm, normed_one, factor_one = layer_norm(mixed, shared[1], shared[2])
+    hidden_in = first_norm.astype(low)
+    inner = mul("rd,zdc->zrc", hidden_in, w_up) + bias_up[:, None, :]
+    active, pull = jax.vjp(partial(jax.nn.gelu, approximate=False), inner)
+    active = active.astype(low)
+    down = jnp.sum(mul("zrc,zoc->zro", active, w_down).astype(low).astype(jnp.float32), axis=0)
+    second = first_norm + down + shared[5]
+    final, normed_two, factor_two = layer_norm(second, shared[3], shared[4])
+    grad_second, grad_gain_two, grad_shift_two = norm_back(upstream, normed_two, factor_two, shared[3])
+    grad_down = grad_second.astype(low)
+    grad_inner = pull(mul("ro,zoc->zrc", grad_down, w_down))[0].astype(low)
+    grad_up_w = mul("rd,zrc->zdc", hidden_in, grad_inner).astype(low)
+    grad_down_w = mul("ro,zrc->zoc", grad_down, active).astype(low)
+    grad_first = grad_second + mul("zrc,zdc->rd", grad_inner, w_up)
+    grad_mixed, grad_gain_one, grad_shift_one = norm_back(grad_first, normed_one, factor_one, shared[1])
+    grad_joined = grad_mixed.astype(low)
+    grad_out_w = mul("ro,zrc->zoc", grad_joined, context).astype(low)
+    grad_context = mul("ro,zoc->zrc", grad_joined, w_out).astype(low).reshape(4, rows, 3, HEAD_DIM)
+    grad_values = mul("zhqk,zqhd->zkhd", probs_low, grad_context).astype(low)
+    grad_probs = mul("zqhd,zkhd->zhqk", grad_context, values)
+    delta = jnp.sum(probs * grad_probs, axis=-1, keepdims=True)
+    grad_scores = (probs * (grad_probs - delta)).astype(low)
+    grad_queries = (mul("zhqk,zkhd->zqhd", grad_scores, keys) * HEAD_DIM**-0.5).astype(low)
+    grad_keys = (mul("zhqk,zqhd->zkhd", grad_scores, queries) * HEAD_DIM**-0.5).astype(low)
+    grad_project = jnp.stack([grad_queries, grad_keys, grad_values], axis=2).reshape(4, rows, 576)
+    grad_project_w = mul("rd,zrc->zdc", rows_in, grad_project).astype(low)
+    grad_layer = grad_mixed + mul("zrc,zdc->rd", grad_project, project)
+    moved = mul("st,sw->tw", pick, grad_layer[text_rows:].astype(low))
+    back = jnp.concatenate([grad_layer[:text_rows] + moved, grad_layer[text_rows:]], axis=0).astype(low)
+
+    attention_grad = jnp.concatenate([grad_project_w, grad_out_w], axis=2)
+    grads = jnp.stack([attention_grad, grad_up_w, grad_down_w], axis=0).reshape(3, 4, 2, 2, 2, 96, 768)
+    small_grad = jnp.concatenate(
+        [
+            jnp.stack(
+                [
+                    jnp.sum(grad_mixed, axis=0),
+                    grad_gain_one,
+                    grad_shift_one,
+                    grad_gain_two,
+                    grad_shift_two,
+                    jnp.sum(grad_second, axis=0),
+                    jnp.sum(grad_queries, axis=1, dtype=jnp.float32).reshape(768),
+                    jnp.sum(grad_values, axis=1, dtype=jnp.float32).reshape(768),
+                ]
+            ),
+            jnp.sum(grad_inner, axis=1, dtype=jnp.float32),
+            jnp.zeros((4, 768), jnp.float32),
+        ],
+        axis=0,
+    )
+    sums, small_sum, text_all, back_all = reduce_all(grads, small_grad, final.astype(low), back)
+    index = lax.axis_index("dp")
+    shared_sum = lax.dynamic_slice(small_sum, (0, index * 96), (6, 96)).T
+    split_sum = jnp.concatenate(
+        [
+            lax.dynamic_slice(small_sum, (6, level * 192), (2, 192)).T,
+            lax.dynamic_slice(small_sum, (8 + level, 0), (1, 768)).reshape(192, 4),
+        ],
+        axis=1,
+    )
+    attention_new = renew(
+        attention_master,
+        attention_moment,
+        attention_average,
+        sums[0].reshape(96, 4, 192),
+        jnp.asarray(ATTENTION_RATES, jnp.float32).reshape(1, 4, 1),
+    )
+    feedforward_new = renew(
+        feedforward_master,
+        feedforward_moment,
+        feedforward_average,
+        jnp.swapaxes(sums[1:], 0, 1),
+        jnp.asarray(FEEDFORWARD_RATES, jnp.float32).reshape(1, 2, 1),
+    )
+    shared_new = renew(shared_master, shared_moment, shared_average, shared_sum, SHARED_RATE)
+    split_new = renew(
+        split_master,
+        split_moment,
+        split_average,
+        split_sum,
+        jnp.asarray(SPLIT_RATES, jnp.float32).reshape(1, 6),
+    )
+    return (
+        text_all.reshape(documents * rows, width),
+        back_all.reshape(documents * rows, width).astype(jnp.float32),
+        *attention_new,
+        *feedforward_new,
+        *shared_new,
+        *split_new,
+    )
+
+
 def solution(mesh):
     in_specs = (
         P("dp", None),
@@ -338,4 +886,5 @@
         P("mp", None),
         P("mp", None),
     )
-    return jax.shard_map(shards, mesh=mesh, in_specs=in_specs, out_specs=out_specs, check_vma=False)
+    body = line_shards if mesh.shape["dp"] == 8 and mesh.shape["mp"] == 4 else general_shards
+    return jax.shard_map(body, mesh=mesh, in_specs=in_specs, out_specs=out_specs, check_vma=False)

time: 737 us -> 524 us (0.71)
  waiting for transfers between devices: 481 us -> 0 us
  Pallas kernels: 0 us -> 316 us
  local copies, waits for them, and re-layouts: 65.1 us -> 40.7 us
  blocking collectives: 23.2 us -> 0 us
  matrix products: 81.4 us -> 96.9 us
  between operations: 15 us -> 1.57 us
    psum x4 -> x0, waiting for transfers between devices: 346 us -> none  [the longest x1 95.2 us: shards(): lax.psum(contract_last(active, feedforward_full[:, 1]).astype(jnp.bfloat1...]
    pallas_call x0 -> x2, Pallas kernels: none -> 316 us  [the longest x1 217 us: reduce_all(): pl.pallas_call(reduce_kernel, out_shape=(jax.ShapeDtypeStruct((3, 96, 768...]
    reduce_scatter x1 -> x0, waiting for transfers between devices: 52.7 us -> none  [shards(): lax.psum_scatter(feedforward_grad, 'dp', scatter_dimension=0, tiled=True)]
    all_gather x2 -> x0, waiting for transfers between devices: 45.1 us -> none  [the longest x1 23.6 us: shards(): lax.all_gather(feedforward_master.astype(jnp.bfloat16), 'dp', axis=0, til...]
    unnamed x11 -> x0, waiting for transfers between devices: 37.2 us -> none
    unnamed x126 -> x124, local copies, waits for them, and re-layouts: 35.9 us -> 8.38 us
    psum x1 -> x0, blocking collectives: 14 us -> none  [shards(): split_sum = lax.psum(split_grad, 'dp')]
    sub x0 -> x1, matrix products: none -> 10.9 us  [line_shards(): raised = jnp.exp(scores - top)]
  transfers between devices with their start and end apart: 9 -> 0, of which waited for: 8 -> 0; matrix products, arithmetic and copies ran while one was open for 10% -> 0% of each run, Pallas kernels for 0% -> 0%
where the time goes in v1:
time: 524 us; the launch traced here: 516 us
  Pallas kernels  316 us (60%)
  matrix products  96.9 us (18%)
  other arithmetic  61.3 us (12%)
  local copies, waits for them, and re-layouts  40.7 us (8%)
    pallas_call x1, Pallas kernels, reduce_all(): pl.pallas_call(reduce_kernel, out_shape=(jax.ShapeDtypeStruct((3, 96, 768...  217 us
    pallas_call x1, Pallas kernels, gather(): pl.pallas_call(gather_kernel, out_shape=(jax.ShapeDtypeStruct((3, 4, 2, 2...  98.3 us
    dot_general x18, matrix products, mul(): return jnp.einsum(form, left, right, preferred_element_type=jnp.float32)  84.5 us
    reduce_sum x2, other arithmetic, layer_norm(): center = value - jnp.mean(value, axis=-1, keepdims=True)  15.4 us
    sub x1, matrix products, line_shards(): raised = jnp.exp(scores - top)  10.9 us

profile of v1, /device:TPU:0, one launch (start us, length us, event | category | flops | bytes accessed | tf_op | source)
XLA Modules:
  0.0 516.2 jit_solution(12329364899671678757)
XLA Ops:
  8.3 98.3 %gather_weights.1 = (bf16[3,4,2,2,2,96,768]{6,5,4,3,2,1,0:T(8,128)(2,1)}, bf16[2,2,2,16,256]{4,3,2,1,0:T(8,128)(2,1)}, bf16[4,16,256]{2,1,0:T(8,128)(2,1)}) custom-call(bf16[3,96,768]{2,1,0:T(8,128)(2,1)} %pad_maximum_fusion.5.own_ref, bf16[16,256]{1,0:T(8,128)(2,1)} %fusion.77.small_ref), custom_call_target="tpu_custom_call" | custom-call | tf_op jit(solution)/shard_map/gather_weights/pallas_call | solution.py:455
  107.6 6.0 %add_convert_fusion = bf16[4,576,512]{2,1,0:T(8,128)(2,1)} fusion(f32[4,576]{1,0:T(4,128)S(1)} %pad_maximum_fusion.7, bf16[3,4,768,768]{3,2,1,0:T(8,128)(2,1)} %bitcast.268, f32[128,768]{1,0:T(8,128)S(1)} %convolution_add_fusion.1, f32[384,768]{1,0:T(8,128)S(1)} %dynamic-slice_convert_fusion), kind=kOutput, calls=%fused_computation.46 | convolution fusion | flops 1815871488 | bytes 7873536 | tf_op jit(solution)/shard_map/rd,zdc->zrc/dot_general | solution.py:741
  114.3 10.9 %fusion.101 = (f32[4,3,512]{2,1,0:T(4,128)S(1)}, f32[4,3,512,512]{2,3,1,0:T(8,128)}) fusion(pred[512]{0:T(512)(128)(4,1)S(1)} %pad_add_fusion, bf16[4,512,3,3,64]{1,4,3,2,0:T(8,128)(2,1)} %bitcast.284), kind=kOutput, calls=%fused_computation.199 | convolution fusion | flops 415236608 | bytes 14180864 | tf_op jit(solution)/shard_map/sub | solution.py:750
  125.3 6.1 %fusion.37 = bf16[4,3,64,512]{3,2,1,0:T(8,128)(2,1)S(1)} fusion(bf16[4,512,3,3,64]{1,4,3,2,0:T(8,128)(2,1)} %bitcast.285, f32[4,3,512,512]{2,3,1,0:T(8,128)} %get-tuple-element.132, f32[4,3,512]{2,1,0:T(4,128)S(1)} %get-tuple-element.131), kind=kOutput, calls=%fused_computation.88 | convolution fusion | flops 409337856 | bytes 14180352 | tf_op jit(solution)/shard_map/zhqk,zkhd->zqhd/dot_general | solution.py:741
  132.2 4.3 convert_reduce_fusion.2
  137.9 13.4 %fusion.99 = (f32[512]{0:T(512)S(1)}, f32[512,768]{1,0:T(8,128)S(1)}) fusion(f32[768]{0:T(1024)S(1)} %add.158, f32[512,768]{1,0:T(8,128)} %convert_reduce_fusion.2, f32[128,768]{1,0:T(8,128)S(1)} %convolution_add_fusion.1, f32[384,768]{1,0:T(8,128)S(1)} %dynamic-slice_convert_fusion), kind=kLoop, calls=%fused_computation.197 | loop fusion | flops 1572352 | bytes 4723712 | tf_op jit(solution)/shard_map/reduce_sum | solution.py:38
  152.3 6.8 %fusion.100 = (bf16[1,4,2,2,2,96,768]{6,5,4,3,2,1,0:T(8,128)(2,1)}, bf16[1,4,2,2,2,96,768]{6,5,4,3,2,1,0:T(8,128)(2,1)S(1)}) fusion(bf16[3,4,2,2,2,96,768]{6,5,4,3,2,1,0:T(8,128)(2,1)} %get-tuple-element.25), kind=kLoop, calls=%fused_computation.198 | loop fusion | bytes 18874368 | tf_op jit(solution)/shard_map/slice | solution.py:724
  159.2 17.4 %fusion.11 = (bf16[4,512,768]{2,1,0:T(8,128)(2,1)S(1)}, f32[4,512,768]{2,1,0:T(8,128)}, f32[4,768,512]{1,2,0:T(8,128)}) fusion(f32[4,768]{1,0:T(4,128)S(1)} %add.165, bf16[4,768,768]{2,1,0:T(8,128)(2,1)S(1)} %bitcast.274, f32[512,768]{1,0:T(8,128)S(1)} %get-tuple-element.121, f32[768]{0:T(1024)S(1)} %add.162, f32[768]{0:T(1024)S(1)} %mul.268, ...), kind=kOutput, calls=%fused_computation.24 | convolution fusion | flops 2521694208 | bytes 22042624 | tf_op jit(solution)/shard_map/rd,zdc->zrc/dot_general | solution.py:741
  176.6 4.1 convert_reduce_fusion.1
  181.4 2.0 fusion.97
  185.1 2.6 multiply_reduce_fusion.1
  190.1 3.5 fusion.95
  193.7 9.7 %convert_reduce_fusion = (f32[4,768]{1,0:T(4,128)}, bf16[4,512,768]{2,1,0:T(8,128)(2,1)S(1)}) fusion(f32[4,512,768]{2,1,0:T(8,128)} %get-tuple-element.119, bf16[4,768,768]{2,1,0:T(8,128)(2,1)} %bitcast.278, f32[512,768]{1,0:T(8,128)S(1)} %get-tuple-element.113, f32[4,768,512]{1,2,0:T(8,128)} %get-tuple-element.133, f32[4,768]{1,0:T(4,128)S(1)} %copy-done.40), kind=kOutput, calls=%fused_computation.25 | convolution fusion | flops 2443047936 | bytes 22044672 | tf_op jit(solution)/shard_map/ro,zoc->zrc/dot_general | solution.py:741
  203.4 3.6 multiply_reduce_fusion.2
  208.2 2.9 convolution_convert_fusion.3
  211.2 5.6 %multiply_reduce_fusion = (f32[4,3,512]{2,1,0:T(4,128)S(1)}, f32[4,3,512,512]{2,3,1,0:T(8,128)}) fusion(f32[4,3,512,512]{2,3,1,0:T(8,128)S(1)} %bitcast.267, f32[4,3,512]{2,1,0:T(4,128)S(1)} %copy-done.28, bf16[4,512,3,64]{1,3,2,0:T(8,128)(2,1)S(1)} %bitcast.293, bf16[4,512,3,3,64]{1,4,3,2,0:T(8,128)(2,1)S(1)} %bitcast.286), kind=kOutput, calls=%fused_computation.3 | convolution fusion | flops 412084224 | bytes 26796032 | tf_op jit(solution)/shard_map/zqhd,zkhd->zhqk/dot_general | solution.py:741
  216.8 7.2 %multiply_convert_fusion = bf16[4,3,512,512]{2,3,1,0:T(8,128)(2,1)S(1)} fusion(f32[4,3,512,512]{2,3,1,0:T(8,128)} %get-tuple-element.136, f32[4,3,512]{2,1,0:T(4,128)S(1)} %get-tuple-element.135, f32[4,3,512,512]{2,3,1,0:T(8,128)S(1)} %bitcast.267, f32[4,3,512]{2,1,0:T(4,128)S(1)} %copy-done.28), kind=kLoop, calls=%fused_computation.2 | loop fusion | flops 12582912 | bytes 31506432 | tf_op jit(solution)/shard_map/convert_element_type | solution.py:777
  225.2 2.0 fusion.47
  227.2 2.7 convert_reduce_fusion.3
  230.4 5.3 %bitcast_add_fusion = f32[512,768]{1,0:T(8,128)S(1)} fusion(f32[512,768]{1,0:T(8,128)S(1)} %get-tuple-element.115, bf16[4,512,576]{1,2,0:T(8,128)(2,1)S(1)} %bitcast.282, bf16[3,4,768,768]{3,2,1,0:T(8,128)(2,1)} %bitcast.271), kind=kOutput, calls=%fused_computation.61 | convolution fusion | flops 1812332544 | bytes 9437184 | tf_op jit(solution)/shard_map/zrc,zdc->rd/dot_general | solution.py:741
  245.4 2.8 concatenate.37.small_ref
  248.2 4.1 convert_bitcast_fusion
  253.1 2.5 pad_maximum_fusion.1
  255.6 6.7 %copy.105 = bf16[4,768,768]{2,1,0:T(8,128)(2,1)} copy(bf16[4,768,768]{1,2,0:T(8,128)(2,1)} %pad_maximum_fusion.1) | data formatting | bytes 9437184 | tf_op jit(solution)/shard_map/concatenate | solution.py:786
  262.3 5.2 %convolution_convert_fusion.1 = bf16[4,768,768]{1,2,0:T(8,128)(2,1)S(1)} fusion(bf16[4,512,768]{2,1,0:T(8,128)(2,1)} %copy-done.51, f32[512,768]{1,0:T(8,128)S(1)} %get-tuple-element.121, f32[768]{0:T(1024)S(1)} %copy-done.38, f32[768]{0:T(1024)S(1)} %copy-done.21, f32[512]{0:T(512)S(1)} %copy-done.31, f32[512]{0:T(512)S(1)} %copy-done.23), kind=kOutput, calls=%fused_computation.56 | convolution fusion | flops 2420244480 | bytes 9447424 | tf_op jit(solution)/shard_map/rd,zrc->zdc/dot_general | solution.py:741
  267.5 3.1 convolution_convert_fusion
  270.6 5.9 %pad_maximum_fusion.grads_ref = bf16[3,4,2,2,2,96,768]{6,5,4,3,2,1,0:T(8,128)(2,1)} fusion(bf16[1,4,2,2,2,96,768]{6,5,4,3,2,1,0:T(8,128)(2,1)S(1)} %bitcast.273, bf16[1,4,2,2,2,96,768]{6,5,4,3,2,1,0:T(8,128)(2,1)S(1)} %bitcast.272, bf16[1,4,2,2,2,96,768]{6,5,4,3,2,1,0:T(8,128)(2,1)S(1)} %bitcast.265), kind=kLoop, calls=%fused_computation.1 | loop fusion | flops 14155776 | bytes 28311552 | tf_op jit(solution)/shard_map/stack | solution.py:787
  276.5 217.3 %reduce_gradients.1 = (f32[3,96,768]{2,1,0:T(8,128)}, f32[16,768]{1,0:T(8,128)}, bf16[3,512,768]{2,1,0:T(8,128)(2,1)}, bf16[3,512,768]{2,1,0:T(8,128)(2,1)}) custom-call(bf16[3,4,2,2,2,96,768]{6,5,4,3,2,1,0:T(8,128)(2,1)} %pad_maximum_fusion.grads_ref, f32[16,768]{1,0:T(8,128)} %concatenate.37.small_ref, bf16[512,768]{1,0:T(8,128)(2,1)} %get-tuple-element.124.text_ref, ...), custom_call_target="tpu_custom_call" | custom-call | tf_op jit(solution)/shard_map/reduce_gradients/pallas_call | solution.py:652
  496.9 4.4 bitcast_convert_fusion
  506.5 2.1 fusion.94
  508.6 2.1 multiply_add_fusion.1
  510.7 2.0 copy.115
  (194 shorter events, 42.0 us)
Async XLA Ops:
  0.7 7.0 %copy-start.25 = (f32[192,6]{0,1:T(8,128)S(1)}, f32[192,6]{0,1:T(8,128)}, u32[]{:S(2)}) copy-start(f32[192,6]{0,1:T(8,128)} %param.34) | copy-start | bytes 13828
  0.7 7.0 %copy-start.35 = (f32[96,6]{0,1:T(8,128)S(1)}, f32[96,6]{0,1:T(8,128)}, u32[]{:S(2)}) copy-start(f32[96,6]{0,1:T(8,128)} %param.31) | copy-start | bytes 6916
  2.7 111.7 %copy-start.45 = (pred[128]{0:T(512)(128)(4,1)}, pred[128]{0:T(512)(128)(4,1)S(1)}, u32[]{:S(2)}) copy-start(pred[128]{0:T(512)(128)(4,1)S(1)} %iota_compare_fusion.3) | copy-start | bytes 388
  5.3 132.6 %copy-start.3 = (f32[384,768]{1,0:T(8,128)}, f32[384,768]{1,0:T(8,128)S(1)}, u32[]{:S(2)}) copy-start(f32[384,768]{1,0:T(8,128)S(1)} %dynamic-slice_convert_fusion) | copy-start | bytes 3538948
  151.4 55.6 %copy-start.22 = (f32[512]{0:T(512)}, f32[512]{0:T(512)S(1)}, u32[]{:S(2)}) copy-start(f32[512]{0:T(512)S(1)} %broadcast_multiply_fusion.5) | copy-start | bytes 6148
  151.7 29.7 %copy-start.29 = (f32[512]{0:T(512)}, f32[512]{0:T(512)S(1)}, u32[]{:S(2)}) copy-start(f32[512]{0:T(512)S(1)} %add_rsqrt_fusion.1) | copy-start | bytes 6148
  152.2 7.0 %copy-start.39 = (f32[4,768]{1,0:T(4,128)}, f32[4,768]{1,0:T(4,128)S(1)}, u32[]{:S(2)}) copy-start(f32[4,768]{1,0:T(4,128)S(1)} %add.165) | copy-start | bytes 36868
  152.3 54.7 %copy-start.20 = (f32[768]{0:T(1024)}, f32[768]{0:T(1024)S(1)}, u32[]{:S(2)}) copy-start(f32[768]{0:T(1024)S(1)} %mul.268) | copy-start | bytes 9220
  152.3 29.0 %copy-start.37 = (f32[768]{0:T(1024)}, f32[768]{0:T(1024)S(1)}, u32[]{:S(2)}) copy-start(f32[768]{0:T(1024)S(1)} %add.162) | copy-start | bytes 9220
  159.2 17.4 %copy-start.4 = (bf16[1,4,2,2,2,96,768]{6,5,4,3,2,1,0:T(8,128)(2,1)}, bf16[1,4,2,2,2,96,768]{6,5,4,3,2,1,0:T(8,128)(2,1)S(1)}, u32[]{:S(2)}) copy-start(bf16[1,4,2,2,2,96,768]{6,5,4,3,2,1,0:T(8,128)(2,1)S(1)} %get-tuple-element.123) | copy-start | bytes 14155780
  159.2 17.4 %copy-start.5 = (bf16[1,4,2,2,2,96,768]{6,5,4,3,2,1,0:T(8,128)(2,1)S(1)}, bf16[1,4,2,2,2,96,768]{6,5,4,3,2,1,0:T(8,128)(2,1)}, u32[]{:S(2)}) copy-start(bf16[1,4,2,2,2,96,768]{6,5,4,3,2,1,0:T(8,128)(2,1)} %get-tuple-element.122) | copy-start | bytes 14155780
  190.1 13.2 %slice-start.3 = ((s8[4718592]{0:T(1024)(128)(4,1)}), s8[4194304]{0:T(1024)(128)(4,1)S(1)}, s32[]{:S(2)}) async-start(s8[4718592]{0:T(1024)(128)(4,1)} %bitcast.275), calls=%async_computation.3 | async-start | bytes 8388608
  193.6 9.7 %copy-start.13 = (f32[512,768]{1,0:T(8,128)}, f32[512,768]{1,0:T(8,128)S(1)}, u32[]{:S(2)}) copy-start(f32[512,768]{1,0:T(8,128)S(1)} %get-tuple-element.113) | copy-start | bytes 4718596
  193.7 9.7 %slice-start.4 = ((s8[4718592]{0:T(1024)(128)(4,1)}), s8[524288]{0:T(1024)(128)(4,1)S(1)}, s32[]{:S(2)}) async-start(s8[4718592]{0:T(1024)(128)(4,1)} %bitcast.275), calls=%async_computation.4 | async-start | bytes 1048576
  193.7 9.7 %copy-start.30 = (f32[512]{0:T(512)S(1)}, f32[512]{0:T(512)}, u32[]{:S(2)}) copy-start(f32[512]{0:T(512)} %copy-done.29) | copy-start | bytes 6148
  193.7 17.5 %slice-start = ((s8[12582912]{0:T(1024)(128)(4,1)}), s8[4194304]{0:T(1024)(128)(4,1)S(1)}, s32[]{:S(2)}) async-start(s8[12582912]{0:T(1024)(128)(4,1)} %bitcast.266), calls=%async_computation | async-start | bytes 8388608
  193.7 17.5 %slice-start.1 = ((s8[12582912]{0:T(1024)(128)(4,1)}), s8[4194304]{0:T(1024)(128)(4,1)S(1)}, s32[]{:S(2)}) async-start(s8[12582912]{0:T(1024)(128)(4,1)} %bitcast.266), calls=%async_computation.1 | async-start | bytes 8388608
  203.4 7.7 %slice-start.2 = ((s8[12582912]{0:T(1024)(128)(4,1)}), s8[4194304]{0:T(1024)(128)(4,1)S(1)}, s32[]{:S(2)}) async-start(s8[12582912]{0:T(1024)(128)(4,1)} %bitcast.266), calls=%async_computation.2 | async-start | bytes 8388608
  230.4 13.9 %copy-start.33 = (f32[768]{0:T(1024)S(1)}, f32[768]{0:T(1024)}, u32[]{:S(2)}) copy-start(f32[768]{0:T(1024)} %get-tuple-element.86) | copy-start | bytes 9220
  230.4 14.4 %copy-start.32 = (f32[768]{0:T(1024)S(1)}, f32[768]{0:T(1024)}, u32[]{:S(2)}) copy-start(f32[768]{0:T(1024)} %get-tuple-element.91) | copy-start | bytes 9220
  255.5 6.7 %copy-start.31 = (f32[512]{0:T(512)S(1)}, f32[512]{0:T(512)}, u32[]{:S(2)}) copy-start(f32[512]{0:T(512)} %copy-done.29) | copy-start | bytes 6148
  255.5 6.7 %copy-start.38 = (f32[768]{0:T(1024)S(1)}, f32[768]{0:T(1024)}, u32[]{:S(2)}) copy-start(f32[768]{0:T(1024)} %copy-done.37) | copy-start | bytes 9220
  276.5 219.1 %copy-start.26 = (f32[192,6]{0,1:T(8,128)S(1)}, f32[192,6]{0,1:T(8,128)}, u32[]{:S(2)}) copy-start(f32[192,6]{0,1:T(8,128)} %param.34) | copy-start | bytes 13828
  276.5 219.1 %copy-start.42 = (f32[192,6]{0,1:T(8,128)S(1)}, f32[192,6]{0,1:T(8,128)}, u32[]{:S(2)}) copy-start(f32[192,6]{0,1:T(8,128)} %param.35) | copy-start | bytes 13828
  276.5 219.1 %copy-start.49 = (f32[6]{0:T(128)S(1)}, f32[6]{0:T(128)}, u32[]{:S(2)}) copy-start(f32[6]{0:T(128)} %constant.147.clone) | copy-start | bytes 76
  276.5 219.8 %copy-start.41 = (f32[192,6]{0,1:T(8,128)S(1)}, f32[192,6]{0,1:T(8,128)}, u32[]{:S(2)}) copy-start(f32[192,6]{0,1:T(8,128)} %param.36) | copy-start | bytes 13828
  503.6 9.1 %copy-start.36 = (f32[96,6]{0,1:T(8,128)S(1)}, f32[96,6]{0,1:T(8,128)}, u32[]{:S(2)}) copy-start(f32[96,6]{0,1:T(8,128)} %param.31) | copy-start | bytes 6916
  503.6 9.1 %copy-start.44 = (f32[96,6]{0,1:T(8,128)S(1)}, f32[96,6]{0,1:T(8,128)}, u32[]{:S(2)}) copy-start(f32[96,6]{0,1:T(8,128)} %param.32) | copy-start | bytes 6916
  503.6 10.4 %copy-start.43 = (f32[96,6]{0,1:T(8,128)S(1)}, f32[96,6]{0,1:T(8,128)}, u32[]{:S(2)}) copy-start(f32[96,6]{0,1:T(8,128)} %param.33) | copy-start | bytes 6916
  503.6 11.0 %copy-start.6 = (bf16[3,512,768]{2,1,0:T(8,128)(2,1)S(1)}, bf16[3,512,768]{2,1,0:T(8,128)(2,1)}, u32[]{:S(2)}) copy-start(bf16[3,512,768]{2,1,0:T(8,128)(2,1)} %get-tuple-element.28) | copy-start | bytes 7077892
  506.4 9.6 %copy-start.1 = (s32[3,128]{1,0:T(4,128)S(1)}, s32[3,128]{1,0:T(4,128)}, u32[]{:S(2)}) copy-start(s32[3,128]{1,0:T(4,128)} %param.21) | copy-start | bytes 4612
  508.6 7.4 %copy-start.12 = (f32[96,4,192]{2,1,0:T(4,128)}, f32[96,4,192]{2,1,0:T(4,128)S(1)}, u32[]{:S(2)}) copy-start(f32[96,4,192]{2,1,0:T(4,128)S(1)} %get-tuple-element.166) | copy-start | bytes 884740
  (27 other events, 121.0 us)
